TPU v7x, 32 devices: a whole 2x2x4 slice. The times are simulated.
32 devices in a mesh: expert: 4 (over y, x), hidden: 8 (over z, core).
Axes of the slice: x: 2, y: 2, z: 4, core: 2. Of those that a mesh axis runs over, the one named last changes fastest.
Arguments:
- tokens: bfloat16 [192, 6144], P(('expert', 'hidden')), may hold values from -6 to 6
- routes: int32 [192, 2], P(('expert', 'hidden')), may hold values from 0 to 3, all different within a row; in each aligned block of 6 rows (0 to 5, 6 to 11, ...) at most 4 rows name the same one
- gate_probs: float32 [192, 2], P(('expert', 'hidden')), may hold values from 0.1 to 1
- cotangent: bfloat16 [192, 6144], P(('expert', 'hidden')), may hold values from -6 to 6
- w_gate: bfloat16 [4, 6144, 8192], P('expert', None, 'hidden'), may hold values from -0.078125 to 0.078125
- w_up: bfloat16 [4, 6144, 8192], P('expert', None, 'hidden'), may hold values from -0.078125 to 0.078125
- w_down: bfloat16 [4, 8192, 6144], P('expert', 'hidden'), may hold values from -0.0625 to 0.0625
Outputs:
- layer_out: bfloat16 [192, 6144], P(('expert', 'hidden'))
- grad_tokens: bfloat16 [192, 6144], P(('expert', 'hidden'))
- grad_gate: bfloat16 [4, 6144, 8192], P('expert', None, 'hidden')
- grad_up: bfloat16 [4, 6144, 8192], P('expert', None, 'hidden')
- grad_down: bfloat16 [4, 8192, 6144], P('expert', 'hidden')
Inputs may be any that keep to these rules, and one draw needn't show every extreme that they name: `routes`: each row names two different experts. Within the tokens of one device (aligned blocks of 6 rows) no expert is named by more than 4 rows, a bound that some block reaches.
All inputs are finite; a program needn't handle non-finite values.
Results may differ from a plain program's by a relative error of at most 0.015.
Values may be sent and summed in bfloat16 or wider, within the bound.
A program may use at most 192 MiB of HBM per device.

v0:
```python
import jax
import jax.numpy as jnp
from jax import lax
from jax.sharding import PartitionSpec as P


def slot_table(route_ids, experts, capacity):
    flat_ids = route_ids.reshape(-1)
    hits = (flat_ids[:, None] == jnp.arange(experts, dtype=jnp.int32)[None, :]).astype(jnp.int32)
    before = jnp.cumsum(hits, axis=0) - hits
    ranks = jnp.sum(before * hits, axis=1)
    slot_ids = flat_ids * capacity + ranks
    table = (slot_ids[:, None] == jnp.arange(experts * capacity, dtype=jnp.int32)[None, :]).astype(
        jnp.float32
    )
    return table.reshape(route_ids.shape[0], 2, experts * capacity)


def on_device(tokens, routes, gate_probs, cotangent, w_gate, w_up, w_down):
    experts = lax.axis_size("expert")
    width = tokens.shape[1]
    capacity = (2 * tokens.shape[0] + experts - 1) // experts + 1
    table = slot_table(routes, experts, capacity)
    placed = jnp.sum(table, axis=1)
    weighted = jnp.sum(table * gate_probs[:, :, None], axis=1)
    send_in = jnp.dot(
        placed.T.astype(jnp.bfloat16), tokens, preferred_element_type=jnp.float32
    ).astype(jnp.bfloat16)
    send_grad = jnp.dot(
        weighted.T, cotangent.astype(jnp.float32), precision=lax.Precision.HIGHEST
    ).astype(jnp.bfloat16)
    send_in = send_in.reshape(experts, capacity, width)
    send_grad = send_grad.reshape(experts, capacity, width)
    grouped = (
        lax.all_gather(send_in[None], "hidden", axis=0, tiled=True),
        lax.all_gather(send_grad[None], "hidden", axis=0, tiled=True),
    )
    arrived = (
        lax.all_to_all(grouped[0], "expert", split_axis=1, concat_axis=1, tiled=True),
        lax.all_to_all(grouped[1], "expert", split_axis=1, concat_axis=1, tiled=True),
    )
    expert_rows = arrived[0].reshape(-1, width)
    grad_rows = arrived[1].reshape(-1, width)
    gate_w = w_gate[0]
    up_w = w_up[0]
    down_w = w_down[0]
    pre_gate = jnp.dot(expert_rows, gate_w, preferred_element_type=jnp.float32)
    pre_up = jnp.dot(expert_rows, up_w, preferred_element_type=jnp.float32)
    sig_gate = jax.nn.sigmoid(pre_gate)
    hidden = (pre_gate * sig_gate * pre_up).astype(jnp.bfloat16)
    summed_out = lax.psum_scatter(
        jnp.dot(hidden, down_w, preferred_element_type=jnp.float32).astype(jnp.bfloat16),
        "hidden",
        scatter_dimension=0,
        tiled=True,
    )
    expert_out = summed_out.reshape(experts, capacity, width)
    returned = lax.all_to_all(expert_out, "expert", split_axis=0, concat_axis=0, tiled=True)
    layer_out = jnp.dot(
        weighted, returned.reshape(-1, width).astype(jnp.float32), precision=lax.Precision.HIGHEST
    ).astype(jnp.bfloat16)
    grad_hidden = jnp.dot(grad_rows, down_w.T, preferred_element_type=jnp.float32)
    grad_pre_gate = (grad_hidden * pre_up * sig_gate * (1.0 + pre_gate * (1.0 - sig_gate))).astype(
        jnp.bfloat16
    )
    grad_pre_up = (grad_hidden * pre_gate * sig_gate).astype(jnp.bfloat16)
    grad_down = jnp.dot(hidden.T, grad_rows, preferred_element_type=jnp.float32).astype(
        jnp.bfloat16
    )
    grad_gate = jnp.dot(expert_rows.T, grad_pre_gate, preferred_element_type=jnp.float32).astype(
        jnp.bfloat16
    )
    grad_up = jnp.dot(expert_rows.T, grad_pre_up, preferred_element_type=jnp.float32).astype(
        jnp.bfloat16
    )
    first = jnp.dot(grad_pre_gate, gate_w.T, preferred_element_type=jnp.float32)
    summed_back = lax.psum_scatter(
        (first + jnp.dot(grad_pre_up, up_w.T, preferred_element_type=jnp.float32)).astype(
            jnp.bfloat16
        ),
        "hidden",
        scatter_dimension=0,
        tiled=True,
    )
    expert_back = summed_back.reshape(experts, capacity, width)
    returned_back = lax.all_to_all(expert_back, "expert", split_axis=0, concat_axis=0, tiled=True)
    grad_tokens = jnp.dot(
        placed,
        returned_back.reshape(-1, width).astype(jnp.float32),
        precision=lax.Precision.HIGHEST,
    ).astype(jnp.bfloat16)
    return (layer_out, grad_tokens, grad_gate[None], grad_up[None], grad_down[None])


def solution(mesh):
    return jax.shard_map(
        on_device,
        mesh=mesh,
        in_specs=(
            P(("expert", "hidden"), None),
            P(("expert", "hidden"), None),
            P(("expert", "hidden"), None),
            P(("expert", "hidden"), None),
            P("expert", None, "hidden"),
            P("expert", None, "hidden"),
            P("expert", "hidden", None),
        ),
        out_specs=(
            P(("expert", "hidden"), None),
            P(("expert", "hidden"), None),
            P("expert", None, "hidden"),
            P("expert", None, "hidden"),
            P("expert", "hidden", None),
        ),
        check_vma=False,
    )
```

profile of v0, /device:TPU:0, one launch (start us, length us, event | category | flops | bytes accessed | tf_op | source)
XLA Modules:
  0.0 226.8 jit_solution(520925246236391324)
XLA Ops:
  7.2 0.8 copy.30
  8.4 0.8 copy.32
  10.3 1.3 convolution_convert_fusion
  12.4 25.8 %all-gather.3.cloned.1.call-done = bf16[8,4,4,6144]{3,2,1,0:T(4,128)(2,1)} async-done(((bf16[1,4,4,6144]{3,2,1,0:T(4,128)(2,1)}), bf16[8,4,4,6144]{3,2,1,0:T(4,128)(2,1)}) %all-gather.3.cloned.1.call-update) | async-done | bytes 1572880 | tf_op jit(solution)/shard_map/all_gather | solution.py:35
  38.2 3.3 %copy.33 = bf16[8,4,4,6144]{3,2,0,1:T(4,128)(2,1)} copy(bf16[8,4,4,6144]{3,2,1,0:T(4,128)(2,1)} %all-gather.3.cloned.1.call-done) | data formatting | bytes 3145728 | tf_op jit(solution)/shard_map/all_gather | solution.py:35
  41.5 3.6 %all-to-all-start = ((bf16[8,4,4,6144]{3,2,0,1:T(4,128)(2,1)}), bf16[8,4,4,6144]{3,2,0,1:T(4,128)(2,1)S(1)}, u32[]{:S(2)}, u32[]{:S(2)}) async-start(bf16[8,4,4,6144]{3,2,0,1:T(4,128)(2,1)} %copy.33), calls=%async_computation | async-start | bytes 3145728 | tf_op jit(solution)/shard_map/all_to_all | solution.py:39
  45.1 19.9 %all-gather.5.cloned.1.call-done = bf16[8,4,4,6144]{3,2,1,0:T(4,128)(2,1)} async-done(((bf16[1,4,4,6144]{3,2,1,0:T(4,128)(2,1)}), bf16[8,4,4,6144]{3,2,1,0:T(4,128)(2,1)}) %all-gather.5.cloned.1.call-update) | async-done | bytes 1572880 | tf_op jit(solution)/shard_map/all_gather | solution.py:36
  65.0 3.3 %copy.35 = bf16[8,4,4,6144]{3,2,0,1:T(4,128)(2,1)} copy(bf16[8,4,4,6144]{3,2,1,0:T(4,128)(2,1)} %all-gather.5.cloned.1.call-done) | data formatting | bytes 3145728 | tf_op jit(solution)/shard_map/all_gather | solution.py:36
  68.3 4.3 %all-to-all-start.2 = ((bf16[8,4,4,6144]{3,2,0,1:T(4,128)(2,1)}), bf16[8,4,4,6144]{3,2,0,1:T(4,128)(2,1)}, u32[]{:S(2)}, u32[]{:S(2)}) async-start(bf16[8,4,4,6144]{3,2,0,1:T(4,128)(2,1)} %copy.35), calls=%async_computation.3 | async-start | bytes 3145728 | tf_op jit(solution)/shard_map/all_to_all | solution.py:40
  72.7 1.9 copy.34
  74.6 2.7 %reshape.48 = bf16[128,6144]{1,0:T(8,128)(2,1)S(1)} reshape(bf16[8,4,4,6144]{3,2,1,0:T(4,128)(2,1)} %copy.34) | data formatting | bytes 3145728 | tf_op jit(solution)/shard_map/reshape | solution.py:42
  77.3 15.4 %all-to-all-done.2 = bf16[8,4,4,6144]{3,2,0,1:T(4,128)(2,1)} async-done(((bf16[8,4,4,6144]{3,2,0,1:T(4,128)(2,1)}), bf16[8,4,4,6144]{3,2,0,1:T(4,128)(2,1)}, u32[]{:S(2)}, u32[]{:S(2)}) %all-to-all-start.2) | async-done | bytes 1572896 | tf_op jit(solution)/shard_map/all_to_all | solution.py:40
  92.6 3.3 %copy.36 = bf16[8,4,4,6144]{3,2,1,0:T(4,128)(2,1)} copy(bf16[8,4,4,6144]{3,2,0,1:T(4,128)(2,1)} %all-to-all-done.2) | data formatting | bytes 3145728 | tf_op jit(solution)/shard_map/all_to_all | solution.py:40
  95.9 2.9 %reshape.51 = bf16[128,6144]{1,0:T(8,128)(2,1)S(1)} reshape(bf16[8,4,4,6144]{3,2,1,0:T(4,128)(2,1)} %copy.36) | data formatting | bytes 3145728 | tf_op jit(solution)/shard_map/reshape | solution.py:43
  98.8 7.2 %fusion.6 = f32[128,1024]{1,0:T(8,128)} fusion(bf16[128,6144]{1,0:T(8,128)(2,1)S(1)} %reshape.48, bf16[1,6144,1024]{2,1,0:T(8,128)(2,1)} %param.12), kind=kOutput, calls=%fused_computation.6 | convolution fusion | flops 1610612736 | bytes 14680064 | tf_op jit(solution)/shard_map/dot_general | solution.py:48
  105.9 9.8 %fusion = f32[128,1024]{1,0:T(8,128)} fusion(bf16[128,6144]{1,0:T(8,128)(2,1)S(1)} %reshape.51, bf16[1,1024,6144]{2,1,0:T(8,128)(2,1)} %param.13), kind=kOutput, calls=%fused_computation | convolution fusion | flops 1610612736 | bytes 14680064 | tf_op jit(solution)/shard_map/dot_general | solution.py:62
  115.7 7.8 %multiply_convert_fusion.1 = (bf16[128,1024]{1,0:T(8,128)(2,1)S(1)}, bf16[128,1024]{1,0:T(8,128)(2,1)}, bf16[128,1024]{1,0:T(8,128)(2,1)}) fusion(f32[128,1024]{1,0:T(8,128)} %fusion, f32[128,1024]{1,0:T(8,128)} %fusion.6, bf16[128,6144]{1,0:T(8,128)(2,1)S(1)} %reshape.48, bf16[1,6144,1024]{2,1,0:T(8,128)(2,1)} %param.11), kind=kOutput, calls=%fused_computation.23 | convolution fusion | flops 1612709888 | bytes 15990784 | tf_op jit(solution)/shard_map/dot_general | solution.py:47
  123.5 6.9 %fusion.4 = f32[128,6144]{1,0:T(8,128)} fusion(bf16[128,1024]{1,0:T(8,128)(2,1)} %get-tuple-element.9, bf16[1,6144,1024]{2,1,0:T(8,128)(2,1)S(1)} %bitcast.49), kind=kOutput, calls=%fused_computation.4 | convolution fusion | flops 1610612736 | bytes 15990784 | tf_op jit(solution)/shard_map/dot_general | solution.py:78
  130.4 11.1 %fusion.15 = bf16[128,6144]{1,0:T(8,128)(2,1)} fusion(f32[128,6144]{1,0:T(8,128)} %fusion.4, bf16[128,1024]{1,0:T(8,128)(2,1)S(1)} %get-tuple-element.7, bf16[1,6144,1024]{2,1,0:T(8,128)(2,1)} %param.11), kind=kOutput, calls=%fused_computation.16 | convolution fusion | flops 1612185600 | bytes 17563648 | tf_op jit(solution)/shard_map/dot_general | solution.py:76
  141.6 7.7 %fusion.18 = bf16[128,6144]{1,0:T(8,128)(2,1)} fusion(bf16[128,1024]{1,0:T(8,128)(2,1)} %get-tuple-element.8, bf16[1,1024,6144]{2,1,0:T(8,128)(2,1)} %param.13), kind=kOutput, calls=%fused_computation.17 | convolution fusion | flops 1611399168 | bytes 14417920 | tf_op jit(solution)/shard_map/dot_general | solution.py:52
  149.2 7.6 %convert_bitcast_fusion.1 = bf16[1,6144,1024]{2,1,0:T(8,128)(2,1)} fusion(bf16[128,6144]{1,0:T(8,128)(2,1)S(1)} %reshape.48, bf16[128,1024]{1,0:T(8,128)(2,1)} %get-tuple-element.9), kind=kOutput, calls=%fused_computation.13 | convolution fusion | flops 1616904192 | bytes 14417920 | tf_op jit(solution)/shard_map/dot_general | solution.py:73
  156.8 6.6 %convert_bitcast_fusion.2 = bf16[1,6144,1024]{2,1,0:T(8,128)(2,1)} fusion(bf16[128,6144]{1,0:T(8,128)(2,1)S(1)} %reshape.48, bf16[128,1024]{1,0:T(8,128)(2,1)S(1)} %get-tuple-element.7), kind=kOutput, calls=%fused_computation.14 | convolution fusion | flops 1616904192 | bytes 14417920 | tf_op jit(solution)/shard_map/dot_general | solution.py:70
  163.4 11.1 %reduce-scatter.5.cloned.1.call-done = bf16[16,6144]{1,0:T(8,128)(2,1)} async-done(((bf16[128,6144]{1,0:T(8,128)(2,1)}), bf16[16,6144]{1,0:T(8,128)(2,1)}) %reduce-scatter.5.cloned.1.call-update) | async-done | bytes 196624 | tf_op jit(solution)/shard_map/reduce_scatter | solution.py:77
  174.6 1.7 reshape.52
  176.3 3.5 %all-to-all-start.3 = ((bf16[4,4,6144]{2,1,0:T(4,128)(2,1)}), bf16[4,4,6144]{2,1,0:T(4,128)(2,1)S(1)}, u32[]{:S(2)}, u32[]{:S(2)}) async-start(bf16[4,4,6144]{2,1,0:T(4,128)(2,1)} %reshape.52), calls=%async_computation.5 | async-start | bytes 393216 | tf_op jit(solution)/shard_map/all_to_all | solution.py:86
  179.8 7.6 %convert_bitcast_fusion = bf16[1,1024,6144]{2,1,0:T(8,128)(2,1)} fusion(bf16[128,1024]{1,0:T(8,128)(2,1)} %get-tuple-element.8, bf16[128,6144]{1,0:T(8,128)(2,1)S(1)} %reshape.51), kind=kOutput, calls=%fused_computation.12 | convolution fusion | flops 1616904192 | bytes 14417920 | tf_op jit(solution)/shard_map/dot_general | solution.py:67
  187.4 21.5 %reduce-scatter.3.cloned.1.call-done = bf16[16,6144]{1,0:T(8,128)(2,1)} async-done(((bf16[128,6144]{1,0:T(8,128)(2,1)}), bf16[16,6144]{1,0:T(8,128)(2,1)}) %reduce-scatter.3.cloned.1.call-update) | async-done | bytes 196624 | tf_op jit(solution)/shard_map/reduce_scatter | solution.py:51
  208.8 1.7 reshape.49
  210.5 3.6 %all-to-all-start.1 = ((bf16[4,4,6144]{2,1,0:T(4,128)(2,1)}), bf16[4,4,6144]{2,1,0:T(4,128)(2,1)S(1)}, u32[]{:S(2)}, u32[]{:S(2)}) async-start(bf16[4,4,6144]{2,1,0:T(4,128)(2,1)} %reshape.49), calls=%async_computation.2 | async-start | bytes 393216 | tf_op jit(solution)/shard_map/all_to_all | solution.py:58
  214.2 0.9 convolution_convert_fusion.2
  215.0 4.3 %all-to-all-done.1 = bf16[4,4,6144]{2,1,0:T(4,128)(2,1)S(1)} async-done(((bf16[4,4,6144]{2,1,0:T(4,128)(2,1)}), bf16[4,4,6144]{2,1,0:T(4,128)(2,1)S(1)}, u32[]{:S(2)}, u32[]{:S(2)}) %all-to-all-start.1) | async-done | bytes 196640 | tf_op jit(solution)/shard_map/all_to_all | solution.py:58
  219.4 0.9 convolution_convert_fusion.3
  (33 shorter events, 2.6 us)
Async XLA Ops:
  7.2 2.1 copy-start
  7.2 31.0 %all-gather.3.cloned.1.call-start = ((), (), s32[]{:S(2)}) async-start(), calls=%async_computation.6 | async-start | bytes 1769472 | tf_op jit(solution)/shard_map/all_gather | solution.py:35
  10.3 54.7 %all-gather.5.cloned.1.call-start = ((), (), s32[]{:S(2)}) async-start(), calls=%async_computation.8 | async-start | bytes 1769472 | tf_op jit(solution)/shard_map/all_gather | solution.py:36
  41.5 26.8 %all-to-all-start = ((bf16[8,4,4,6144]{3,2,0,1:T(4,128)(2,1)}), bf16[8,4,4,6144]{3,2,0,1:T(4,128)(2,1)S(1)}, u32[]{:S(2)}, u32[]{:S(2)}) async-start(bf16[8,4,4,6144]{3,2,0,1:T(4,128)(2,1)} %copy.33), calls=%async_computation | async-start | bytes 3145728 | tf_op jit(solution)/shard_map/all_to_all | solution.py:39
  68.3 24.3 %all-to-all-start.2 = ((bf16[8,4,4,6144]{3,2,0,1:T(4,128)(2,1)}), bf16[8,4,4,6144]{3,2,0,1:T(4,128)(2,1)}, u32[]{:S(2)}, u32[]{:S(2)}) async-start(bf16[8,4,4,6144]{3,2,0,1:T(4,128)(2,1)} %copy.35), calls=%async_computation.3 | async-start | bytes 3145728 | tf_op jit(solution)/shard_map/all_to_all | solution.py:40
  72.6 101.9 %reduce-scatter.5.cloned.1.call-start = ((), (), s32[]{:S(2)}) async-start(), calls=%async_computation.9 | async-start | bytes 1769472 | tf_op jit(solution)/shard_map/reduce_scatter | solution.py:77
  105.9 17.6 %slice-start = ((s8[12582912]{0:T(1024)(128)(4,1)}), s8[4194304]{0:T(1024)(128)(4,1)S(1)}, s32[]{:S(2)}) async-start(s8[12582912]{0:T(1024)(128)(4,1)} %bitcast.48), calls=%async_computation.10 | async-start | bytes 8388608
  105.9 17.6 %slice-start.1 = ((s8[12582912]{0:T(1024)(128)(4,1)}), s8[4194304]{0:T(1024)(128)(4,1)S(1)}, s32[]{:S(2)}) async-start(s8[12582912]{0:T(1024)(128)(4,1)} %bitcast.48), calls=%async_computation.11 | async-start | bytes 8388608
  115.7 7.8 %slice-start.2 = ((s8[12582912]{0:T(1024)(128)(4,1)}), s8[4194304]{0:T(1024)(128)(4,1)S(1)}, s32[]{:S(2)}) async-start(s8[12582912]{0:T(1024)(128)(4,1)} %bitcast.48), calls=%async_computation.12 | async-start | bytes 8388608
  141.5 67.3 %reduce-scatter.3.cloned.1.call-start = ((), (), s32[]{:S(2)}) async-start(), calls=%async_computation.7 | async-start | bytes 1769472 | tf_op jit(solution)/shard_map/reduce_scatter | solution.py:51
  176.3 34.3 %all-to-all-start.3 = ((bf16[4,4,6144]{2,1,0:T(4,128)(2,1)}), bf16[4,4,6144]{2,1,0:T(4,128)(2,1)S(1)}, u32[]{:S(2)}, u32[]{:S(2)}) async-start(bf16[4,4,6144]{2,1,0:T(4,128)(2,1)} %reshape.52), calls=%async_computation.5 | async-start | bytes 393216 | tf_op jit(solution)/shard_map/all_to_all | solution.py:86
  179.7 40.5 %copy-start.1 = (bf16[6,6144]{1,0:T(8,128)(2,1)S(1)}, bf16[6,6144]{1,0:T(8,128)(2,1)}, u32[]{:S(2)}) copy-start(bf16[6,6144]{1,0:T(8,128)(2,1)} %param.7) | copy-start | bytes 221188
  210.5 8.8 %all-to-all-start.1 = ((bf16[4,4,6144]{2,1,0:T(4,128)(2,1)}), bf16[4,4,6144]{2,1,0:T(4,128)(2,1)S(1)}, u32[]{:S(2)}, u32[]{:S(2)}) async-start(bf16[4,4,6144]{2,1,0:T(4,128)(2,1)} %reshape.49), calls=%async_computation.2 | async-start | bytes 393216 | tf_op jit(solution)/shard_map/all_to_all | solution.py:58
Sparse Core Ops, SparseCore 0:
  10.4 27.7 all-gather.2
  40.4 24.5 all-gather.4
  141.6 32.8 reduce-scatter.4
  176.7 32.0 reduce-scatter.2
where the time goes:
time: 228 us; the launch traced here: 227 us
  waiting for transfers between devices  98 us (43%)
  matrix products  75.4 us (33%)
  local copies, waits for them, and re-layouts  23.9 us (10%)
  starting transfers between devices  15.3 us (7%)
  between operations  13.9 us (6%)
    all_gather x1, waiting for transfers between devices, on_device(): lax.all_gather(send_in[None], 'hidden', axis=0, tiled=True)  25.8 us
    reduce_scatter x1, waiting for transfers between devices, on_device(): lax.psum_scatter(jnp.dot(hidden, down_w, preferred_element_type=jnp.float...  21.5 us
    all_gather x1, waiting for transfers between devices, on_device(): lax.all_gather(send_grad[None], 'hidden', axis=0, tiled=True)  19.9 us
    all_to_all x1, waiting for transfers between devices, on_device(): lax.all_to_all(grouped[1], 'expert', split_axis=1, concat_axis=1, tiled=T...  15.4 us
    reduce_scatter x1, waiting for transfers between devices, on_device(): lax.psum_scatter((first + jnp.dot(grad_pre_up, up_w.T, preferred_element_...  11.1 us
    dot_general x1, matrix products, on_device(): first = jnp.dot(grad_pre_gate, gate_w.T, preferred_element_type=jnp.float32)  11.1 us
    dot_general x1, matrix products, on_device(): jnp.dot(grad_rows, down_w.T, preferred_element_type=jnp.float32)  9.76 us
    dot_general x1, matrix products, on_device(): pre_gate = jnp.dot(expert_rows, gate_w, preferred_element_type=jnp.float32)  7.78 us
  transfers between devices with their start and end apart: 8, of which 6 were waited for; matrix products, arithmetic and copies ran while one was open for 21% of the time, Pallas kernels for 0%

commit v1 on v0

--- a/solution.py
+++ b/solution.py
@@ -1,7 +1,41 @@
+import functools
 import jax
 import jax.numpy as jnp
 from jax import lax
 from jax.sharding import PartitionSpec as P
+
+
+def fit_the_corner(view, shard_axis):
+    inter, block_last, formed = (
+        lax.axis_size(shard_axis),
+        lax.axis_index(shard_axis),
+        view.shape[0],
+    )
+    vals = [dd * inter if dev == 0 else dd for dev, dd in enumerate(view.shape)]
+    part_next = lax.dynamic_update_slice_in_dim(
+        jnp.zeros(vals, view.dtype), view, block_last * formed, axis=0
+    )
+    step_out = f_now = view
+    for s in range(1, inter // 2 + 1):
+        step_out = lax.ppermute(
+            step_out, shard_axis, list(map(lambda dev: (dev, (dev + 1) % inter), range(inter)))
+        )
+        part_next = lax.dynamic_update_slice_in_dim(
+            part_next, step_out, (block_last - s) % inter * formed, axis=0
+        )
+        if 2 * s < inter:
+            f_now = lax.ppermute(
+                f_now,
+                shard_axis,
+                perm=list(map(lambda dev: (dev, (dev - 1) % inter), range(inter))),
+            )
+            part_next = lax.dynamic_update_slice_in_dim(
+                part_next, f_now, (block_last + s) % inter * formed, axis=0
+            )
+    return part_next
+
+
+hold_vectors = functools.partial(fit_the_corner, shard_axis="hidden")
 
 
 def slot_table(route_ids, experts, capacity):
@@ -33,7 +67,7 @@
     send_grad = send_grad.reshape(experts, capacity, width)
     grouped = (
         lax.all_gather(send_in[None], "hidden", axis=0, tiled=True),
-        lax.all_gather(send_grad[None], "hidden", axis=0, tiled=True),
+        hold_vectors(send_grad[None]),
     )
     arrived = (
         lax.all_to_all(grouped[0], "expert", split_axis=1, concat_axis=1, tiled=True),

time: 228 us -> 217 us (0.952)
  waiting for transfers between devices: 98 us -> 75.2 us
  starting transfers between devices: 15.3 us -> 28 us
    all_gather x1, waiting for transfers between devices: 25.8 us -> 0.01 us  [on_device(): lax.all_gather(send_in[None], 'hidden', axis=0, tiled=True)]
    reduce_scatter x1, waiting for transfers between devices: 21.5 us -> 1.51 us  [on_device(): lax.psum_scatter(jnp.dot(hidden, down_w, preferred_element_type=jnp.float...]
    all_gather x1 -> x0, waiting for transfers between devices: 19.9 us -> none  [on_device(): lax.all_gather(send_grad[None], 'hidden', axis=0, tiled=True)]
    all_to_all x1, waiting for transfers between devices: 0.01 us -> 17.4 us  [on_device(): lax.all_to_all(grouped[0], 'expert', split_axis=1, concat_axis=1, tiled=T...]
    ppermute x0 -> x7, waiting for transfers between devices: none -> 16.6 us  [the longest x4 10.3 us: fit_the_corner(): lax.ppermute(step_out, shard_axis, list(map(lambda dev: (dev, (dev + 1) %...]
    ppermute x0 -> x7, starting transfers between devices: none -> 11.9 us  [the longest x3 11.4 us: fit_the_corner(): lax.ppermute(f_now, shard_axis, perm=list(map(lambda dev: (dev, (dev - 1)...]
    reduce_scatter x1, waiting for transfers between devices: 11.1 us -> 21.9 us  [on_device(): lax.psum_scatter((first + jnp.dot(grad_pre_up, up_w.T, preferred_element_...]
    dynamic_update_slice x0 -> x8, local copies, waits for them, and re-layouts: none -> 5.96 us  [the longest x4 2.98 us: fit_the_corner(): lax.dynamic_update_slice_in_dim(part_next, step_out, (block_last - s) % i...]
  transfers between devices with their start and end apart: 8 -> 14, of which waited for: 6 -> 10; matrix products, arithmetic and copies ran while one was open for 21% -> 27% of each run, Pallas kernels for 0% -> 0%
where the time goes in v1:
time: 217 us; the launch traced here: 216 us
  waiting for transfers between devices  75.2 us (35%)
  matrix products  73.9 us (34%)
  starting transfers between devices  28 us (13%)
  local copies, waits for them, and re-layouts  24.8 us (11%)
  between operations  13.9 us (6%)
    reduce_scatter x1, waiting for transfers between devices, on_device(): lax.psum_scatter((first + jnp.dot(grad_pre_up, up_w.T, preferred_element_...  21.9 us
    all_to_all x1, waiting for transfers between devices, on_device(): lax.all_to_all(grouped[0], 'expert', split_axis=1, concat_axis=1, tiled=T...  17.4 us
    all_to_all x1, waiting for transfers between devices, on_device(): lax.all_to_all(grouped[1], 'expert', split_axis=1, concat_axis=1, tiled=T...  13.5 us
    ppermute x3, starting transfers between devices, fit_the_corner(): lax.ppermute(f_now, shard_axis, perm=list(map(lambda dev: (dev, (dev - 1)...  11.4 us
    ppermute x4, waiting for transfers between devices, fit_the_corner(): lax.ppermute(step_out, shard_axis, list(map(lambda dev: (dev, (dev + 1) %...  10.3 us
    dot_general x1, matrix products, on_device(): first = jnp.dot(grad_pre_gate, gate_w.T, preferred_element_type=jnp.float32)  10.1 us
    dot_general x1, matrix products, on_device(): jnp.dot(grad_rows, down_w.T, preferred_element_type=jnp.float32)  9.63 us
    dot_general x1, matrix products, on_device(): jnp.dot(grad_pre_up, up_w.T, preferred_element_type=jnp.float32)  8.82 us
  transfers between devices with their start and end apart: 14, of which 10 were waited for; matrix products, arithmetic and copies ran while one was open for 27% of the time, Pallas kernels for 0%

profile of v1, /device:TPU:0, one launch (start us, length us, event | category | flops | bytes accessed | tf_op | source)
XLA Modules:
  0.0 216.1 jit_solution(9520843341958039542)
XLA Ops:
  10.3 4.1 %collective-permute-start.1 = (bf16[1,4,4,6144]{3,2,0,1:T(4,128)(2,1)S(1)}, bf16[1,4,4,6144]{3,2,0,1:T(4,128)(2,1)S(1)}, u32[]{:S(2)}, u32[]{:S(2)}) collective-permute-start(bf16[1,4,4,6144]{3,2,0,1:T(4,128)(2,1)S(1)} %bitcast.53), channel_id=1, source_target_pairs={{0,7},{1,0},{2,1},{3,2},{4,3},{5,4},{6,5},{7,6},{8,15},{9,8},{10,9... | collective-permute-start | bytes 589832 | tf_op jit(solution)/shard_map/ppermute | solution.py:27
  16.3 1.9 broadcast_in_dim.16
  18.9 3.5 %collective-permute-start.3 = (bf16[1,4,4,6144]{3,2,0,1:T(4,128)(2,1)S(1)}, bf16[1,4,4,6144]{3,2,0,1:T(4,128)(2,1)S(1)}, u32[]{:S(2)}, u32[]{:S(2)}) collective-permute-start(bf16[1,4,4,6144]{3,2,0,1:T(4,128)(2,1)S(1)} %collective-permute-done.1), channel_id=1, source_target_pairs={{0,7},{1,0},{2,1},{3,2},{4,3},{5,4},{6,5},{7,6},{8,15},{9,8},{10,9... | collective-permute-start | bytes 589832 | tf_op jit(solution)/shard_map/ppermute | solution.py:27
  23.9 2.2 %collective-permute-done.2 = bf16[1,4,4,6144]{3,2,0,1:T(4,128)(2,1)S(1)} collective-permute-done((bf16[1,4,4,6144]{3,2,0,1:T(4,128)(2,1)S(1)}, bf16[1,4,4,6144]{3,2,0,1:T(4,128)(2,1)S(1)}, u32[]{:S(2)}, u32[]{:S(2)}) %collective-permute-start.2) | collective-permute-done | bytes 196640 | tf_op jit(solution)/shard_map/ppermute | solution.py:20
  26.2 3.5 %collective-permute-done.3 = bf16[1,4,4,6144]{3,2,0,1:T(4,128)(2,1)S(1)} collective-permute-done((bf16[1,4,4,6144]{3,2,0,1:T(4,128)(2,1)S(1)}, bf16[1,4,4,6144]{3,2,0,1:T(4,128)(2,1)S(1)}, u32[]{:S(2)}, u32[]{:S(2)}) %collective-permute-start.3) | collective-permute-done | bytes 196640 | tf_op jit(solution)/shard_map/ppermute | solution.py:27
  29.7 3.7 %collective-permute-start.5 = (bf16[1,4,4,6144]{3,2,0,1:T(4,128)(2,1)S(1)}, bf16[1,4,4,6144]{3,2,0,1:T(4,128)(2,1)S(1)}, u32[]{:S(2)}, u32[]{:S(2)}) collective-permute-start(bf16[1,4,4,6144]{3,2,0,1:T(4,128)(2,1)S(1)} %collective-permute-done.3), channel_id=1, source_target_pairs={{0,7},{1,0},{2,1},{3,2},{4,3},{5,4},{6,5},{7,6},{8,15},{9,8},{10,9... | collective-permute-start | bytes 589832 | tf_op jit(solution)/shard_map/ppermute | solution.py:27
  34.9 4.3 %collective-permute-done.4 = bf16[1,4,4,6144]{3,2,0,1:T(4,128)(2,1)S(1)} collective-permute-done((bf16[1,4,4,6144]{3,2,0,1:T(4,128)(2,1)S(1)}, bf16[1,4,4,6144]{3,2,0,1:T(4,128)(2,1)S(1)}, u32[]{:S(2)}, u32[]{:S(2)}) %collective-permute-start.4) | collective-permute-done | bytes 196640 | tf_op jit(solution)/shard_map/ppermute | solution.py:20
  40.0 2.8 %collective-permute-done.5 = bf16[1,4,4,6144]{3,2,0,1:T(4,128)(2,1)S(1)} collective-permute-done((bf16[1,4,4,6144]{3,2,0,1:T(4,128)(2,1)S(1)}, bf16[1,4,4,6144]{3,2,0,1:T(4,128)(2,1)S(1)}, u32[]{:S(2)}, u32[]{:S(2)}) %collective-permute-start.5) | collective-permute-done | bytes 196640 | tf_op jit(solution)/shard_map/ppermute | solution.py:27
  43.5 3.8 %collective-permute-done.6 = bf16[1,4,4,6144]{3,2,0,1:T(4,128)(2,1)S(1)} collective-permute-done((bf16[1,4,4,6144]{3,2,0,1:T(4,128)(2,1)S(1)}, bf16[1,4,4,6144]{3,2,0,1:T(4,128)(2,1)S(1)}, u32[]{:S(2)}, u32[]{:S(2)}) %collective-permute-start.6) | collective-permute-done | bytes 196640 | tf_op jit(solution)/shard_map/ppermute | solution.py:20
  48.0 4.2 %all-to-all-start.2 = ((bf16[8,4,4,6144]{3,2,0,1:T(4,128)(2,1)}), bf16[8,4,4,6144]{3,2,0,1:T(4,128)(2,1)S(1)}, u32[]{:S(2)}, u32[]{:S(2)}) async-start(bf16[8,4,4,6144]{3,2,0,1:T(4,128)(2,1)} %constant_dynamic-update-slice_fusion), calls=%async_computation.3 | async-start | bytes 3145728 | tf_op jit(solution)/shard_map/all_to_all | solution.py:74
  52.2 3.3 %copy.37 = bf16[8,4,4,6144]{3,2,0,1:T(4,128)(2,1)} copy(bf16[8,4,4,6144]{3,2,1,0:T(4,128)(2,1)} %all-gather.2.cloned.1.call-done) | data formatting | bytes 3145728 | tf_op jit(solution)/shard_map/all_gather | solution.py:69
  55.5 13.5 %all-to-all-done.2 = bf16[8,4,4,6144]{3,2,0,1:T(4,128)(2,1)S(1)} async-done(((bf16[8,4,4,6144]{3,2,0,1:T(4,128)(2,1)}), bf16[8,4,4,6144]{3,2,0,1:T(4,128)(2,1)S(1)}, u32[]{:S(2)}, u32[]{:S(2)}) %all-to-all-start.2) | async-done | bytes 1572896 | tf_op jit(solution)/shard_map/all_to_all | solution.py:74
  69.0 4.3 %all-to-all-start = ((bf16[8,4,4,6144]{3,2,0,1:T(4,128)(2,1)}), bf16[8,4,4,6144]{3,2,0,1:T(4,128)(2,1)}, u32[]{:S(2)}, u32[]{:S(2)}) async-start(bf16[8,4,4,6144]{3,2,0,1:T(4,128)(2,1)} %copy.37), calls=%async_computation | async-start | bytes 3145728 | tf_op jit(solution)/shard_map/all_to_all | solution.py:73
  74.6 17.4 %all-to-all-done = bf16[8,4,4,6144]{3,2,0,1:T(4,128)(2,1)} async-done(((bf16[8,4,4,6144]{3,2,0,1:T(4,128)(2,1)}), bf16[8,4,4,6144]{3,2,0,1:T(4,128)(2,1)}, u32[]{:S(2)}, u32[]{:S(2)}) %all-to-all-start) | async-done | bytes 1572896 | tf_op jit(solution)/shard_map/all_to_all | solution.py:73
  92.1 3.3 %copy.38 = bf16[8,4,4,6144]{3,2,1,0:T(4,128)(2,1)} copy(bf16[8,4,4,6144]{3,2,0,1:T(4,128)(2,1)} %all-to-all-done) | data formatting | bytes 3145728 | tf_op jit(solution)/shard_map/all_to_all | solution.py:73
  95.3 2.7 %reshape.48 = bf16[128,6144]{1,0:T(8,128)(2,1)S(1)} reshape(bf16[8,4,4,6144]{3,2,1,0:T(4,128)(2,1)} %copy.38) | data formatting | bytes 3145728 | tf_op jit(solution)/shard_map/reshape | solution.py:76
  98.0 6.4 %fusion.6 = f32[128,1024]{1,0:T(8,128)S(1)} fusion(bf16[128,6144]{1,0:T(8,128)(2,1)S(1)} %reshape.48, bf16[1,6144,1024]{2,1,0:T(8,128)(2,1)} %param.12), kind=kOutput, calls=%fused_computation.6 | convolution fusion | flops 1610612736 | bytes 14680064 | tf_op jit(solution)/shard_map/dot_general | solution.py:82
  104.4 6.4 %fusion.10 = f32[128,1024]{1,0:T(8,128)S(1)} fusion(bf16[128,6144]{1,0:T(8,128)(2,1)S(1)} %reshape.48, bf16[1,6144,1024]{2,1,0:T(8,128)(2,1)} %param.11), kind=kOutput, calls=%fused_computation.10 | convolution fusion | flops 1610612736 | bytes 14680064 | tf_op jit(solution)/shard_map/dot_general | solution.py:81
  110.8 9.6 %multiply_convert_fusion.1 = (bf16[128,1024]{1,0:T(8,128)(2,1)}, bf16[128,1024]{1,0:T(8,128)(2,1)S(1)}, bf16[128,1024]{1,0:T(8,128)(2,1)S(1)}) fusion(f32[128,1024]{1,0:T(8,128)S(1)} %fusion.10, f32[128,1024]{1,0:T(8,128)S(1)} %fusion.6, bf16[128,6144]{1,0:T(8,128)(2,1)S(1)} %reshape.51, bf16[1,1024,6144]{2,1,0:T(8,128)(2,1)} %param.13), kind=kOutput, calls=%fused_computation.23 | convolution fusion | flops 1612709888 | bytes 15990784 | tf_op jit(solution)/shard_map/dot_general | solution.py:96
  121.1 7.5 %fusion.18 = bf16[128,6144]{1,0:T(8,128)(2,1)} fusion(bf16[128,1024]{1,0:T(8,128)(2,1)S(1)} %get-tuple-element.8, bf16[1,1024,6144]{2,1,0:T(8,128)(2,1)} %param.13), kind=kOutput, calls=%fused_computation.17 | convolution fusion | flops 1611399168 | bytes 14417920 | tf_op jit(solution)/shard_map/dot_general | solution.py:86
  128.9 8.8 %fusion.4 = f32[128,6144]{1,0:T(8,128)S(1)} fusion(bf16[128,1024]{1,0:T(8,128)(2,1)S(1)} %get-tuple-element.9, bf16[1,6144,1024]{2,1,0:T(8,128)(2,1)} %param.12), kind=kOutput, calls=%fused_computation.4 | convolution fusion | flops 1610612736 | bytes 15990784 | tf_op jit(solution)/shard_map/dot_general | solution.py:112
  137.8 10.1 %fusion.15 = bf16[128,6144]{1,0:T(8,128)(2,1)} fusion(f32[128,6144]{1,0:T(8,128)S(1)} %fusion.4, bf16[128,1024]{1,0:T(8,128)(2,1)S(1)} %copy-done.2, bf16[1,6144,1024]{2,1,0:T(8,128)(2,1)} %param.11), kind=kOutput, calls=%fused_computation.16 | convolution fusion | flops 1612185600 | bytes 17563648 | tf_op jit(solution)/shard_map/dot_general | solution.py:110
  147.9 7.6 %convert_bitcast_fusion.2 = bf16[1,6144,1024]{2,1,0:T(8,128)(2,1)} fusion(bf16[128,6144]{1,0:T(8,128)(2,1)S(1)} %reshape.48, bf16[128,1024]{1,0:T(8,128)(2,1)} %get-tuple-element.7), kind=kOutput, calls=%fused_computation.14 | convolution fusion | flops 1616904192 | bytes 14417920 | tf_op jit(solution)/shard_map/dot_general | solution.py:104
  155.5 6.6 %convert_bitcast_fusion.1 = bf16[1,6144,1024]{2,1,0:T(8,128)(2,1)} fusion(bf16[128,6144]{1,0:T(8,128)(2,1)S(1)} %reshape.48, bf16[128,1024]{1,0:T(8,128)(2,1)S(1)} %get-tuple-element.9), kind=kOutput, calls=%fused_computation.13 | convolution fusion | flops 1616904192 | bytes 14417920 | tf_op jit(solution)/shard_map/dot_general | solution.py:107
  162.1 1.5 reduce-scatter.3.cloned.1.call-done
  163.6 1.7 reshape.49
  165.3 3.6 %all-to-all-start.1 = ((bf16[4,4,6144]{2,1,0:T(4,128)(2,1)}), bf16[4,4,6144]{2,1,0:T(4,128)(2,1)S(1)}, u32[]{:S(2)}, u32[]{:S(2)}) async-start(bf16[4,4,6144]{2,1,0:T(4,128)(2,1)} %reshape.49), calls=%async_computation.2 | async-start | bytes 393216 | tf_op jit(solution)/shard_map/all_to_all | solution.py:92
  168.8 7.6 %convert_bitcast_fusion = bf16[1,1024,6144]{2,1,0:T(8,128)(2,1)} fusion(bf16[128,1024]{1,0:T(8,128)(2,1)} %copy-done.3, bf16[128,6144]{1,0:T(8,128)(2,1)S(1)} %reshape.51), kind=kOutput, calls=%fused_computation.12 | convolution fusion | flops 1616904192 | bytes 14417920 | tf_op jit(solution)/shard_map/dot_general | solution.py:101
  176.4 21.9 %reduce-scatter.5.cloned.1.call-done = bf16[16,6144]{1,0:T(8,128)(2,1)} async-done(((bf16[128,6144]{1,0:T(8,128)(2,1)}), bf16[16,6144]{1,0:T(8,128)(2,1)}) %reduce-scatter.5.cloned.1.call-update) | async-done | bytes 196624 | tf_op jit(solution)/shard_map/reduce_scatter | solution.py:111
  198.3 1.7 reshape.52
  200.0 3.4 %all-to-all-start.3 = ((bf16[4,4,6144]{2,1,0:T(4,128)(2,1)}), bf16[4,4,6144]{2,1,0:T(4,128)(2,1)S(1)}, u32[]{:S(2)}, u32[]{:S(2)}) async-start(bf16[4,4,6144]{2,1,0:T(4,128)(2,1)} %reshape.52), calls=%async_computation.5 | async-start | bytes 393216 | tf_op jit(solution)/shard_map/all_to_all | solution.py:120
  204.4 4.3 %all-to-all-done.3 = bf16[4,4,6144]{2,1,0:T(4,128)(2,1)S(1)} async-done(((bf16[4,4,6144]{2,1,0:T(4,128)(2,1)}), bf16[4,4,6144]{2,1,0:T(4,128)(2,1)S(1)}, u32[]{:S(2)}, u32[]{:S(2)}) %all-to-all-start.3) | async-done | bytes 196640 | tf_op jit(solution)/shard_map/all_to_all | solution.py:120
  (49 shorter events, 15.1 us)
Async XLA Ops:
  7.2 2.1 copy-start
  7.2 45.1 %all-gather.2.cloned.1.call-start = ((), (), s32[]{:S(2)}) async-start(), calls=%async_computation.6 | async-start | bytes 1769472 | tf_op jit(solution)/shard_map/all_gather | solution.py:69
  9.8 9.1 %collective-permute-start = (bf16[1,4,4,6144]{3,2,0,1:T(4,128)(2,1)S(1)}, bf16[1,4,4,6144]{3,2,0,1:T(4,128)(2,1)S(1)}, u32[]{:S(2)}, u32[]{:S(2)}) collective-permute-start(bf16[1,4,4,6144]{3,2,0,1:T(4,128)(2,1)S(1)} %bitcast.52), channel_id=1, source_target_pairs={{0,1},{1,2},{2,3},{3,4},{4,5},{5,6},{6,7},{7,0},{8,9},{9,10},{10,1... | collective-permute-start | bytes 589832 | tf_op jit(solution)/shard_map/ppermute | solution.py:20
  10.3 8.6 %collective-permute-start.1 = (bf16[1,4,4,6144]{3,2,0,1:T(4,128)(2,1)S(1)}, bf16[1,4,4,6144]{3,2,0,1:T(4,128)(2,1)S(1)}, u32[]{:S(2)}, u32[]{:S(2)}) collective-permute-start(bf16[1,4,4,6144]{3,2,0,1:T(4,128)(2,1)S(1)} %bitcast.53), channel_id=1, source_target_pairs={{0,7},{1,0},{2,1},{3,2},{4,3},{5,4},{6,5},{7,6},{8,15},{9,8},{10,9... | collective-permute-start | bytes 589832 | tf_op jit(solution)/shard_map/ppermute | solution.py:27
  18.9 7.3 %collective-permute-start.2 = (bf16[1,4,4,6144]{3,2,0,1:T(4,128)(2,1)S(1)}, bf16[1,4,4,6144]{3,2,0,1:T(4,128)(2,1)S(1)}, u32[]{:S(2)}, u32[]{:S(2)}) collective-permute-start(bf16[1,4,4,6144]{3,2,0,1:T(4,128)(2,1)S(1)} %collective-permute-done), channel_id=1, source_target_pairs={{0,1},{1,2},{2,3},{3,4},{4,5},{5,6},{6,7},{7,0},{8,9},{9,10},{10,1... | collective-permute-start | bytes 589832 | tf_op jit(solution)/shard_map/ppermute | solution.py:20
  18.9 10.8 %collective-permute-start.3 = (bf16[1,4,4,6144]{3,2,0,1:T(4,128)(2,1)S(1)}, bf16[1,4,4,6144]{3,2,0,1:T(4,128)(2,1)S(1)}, u32[]{:S(2)}, u32[]{:S(2)}) collective-permute-start(bf16[1,4,4,6144]{3,2,0,1:T(4,128)(2,1)S(1)} %collective-permute-done.1), channel_id=1, source_target_pairs={{0,7},{1,0},{2,1},{3,2},{4,3},{5,4},{6,5},{7,6},{8,15},{9,8},{10,9... | collective-permute-start | bytes 589832 | tf_op jit(solution)/shard_map/ppermute | solution.py:27
  26.2 13.1 %collective-permute-start.4 = (bf16[1,4,4,6144]{3,2,0,1:T(4,128)(2,1)S(1)}, bf16[1,4,4,6144]{3,2,0,1:T(4,128)(2,1)S(1)}, u32[]{:S(2)}, u32[]{:S(2)}) collective-permute-start(bf16[1,4,4,6144]{3,2,0,1:T(4,128)(2,1)S(1)} %collective-permute-done.2), channel_id=1, source_target_pairs={{0,1},{1,2},{2,3},{3,4},{4,5},{5,6},{6,7},{7,0},{8,9},{9,10},{10,1... | collective-permute-start | bytes 589832 | tf_op jit(solution)/shard_map/ppermute | solution.py:20
  29.7 13.1 %collective-permute-start.5 = (bf16[1,4,4,6144]{3,2,0,1:T(4,128)(2,1)S(1)}, bf16[1,4,4,6144]{3,2,0,1:T(4,128)(2,1)S(1)}, u32[]{:S(2)}, u32[]{:S(2)}) collective-permute-start(bf16[1,4,4,6144]{3,2,0,1:T(4,128)(2,1)S(1)} %collective-permute-done.3), channel_id=1, source_target_pairs={{0,7},{1,0},{2,1},{3,2},{4,3},{5,4},{6,5},{7,6},{8,15},{9,8},{10,9... | collective-permute-start | bytes 589832 | tf_op jit(solution)/shard_map/ppermute | solution.py:27
  39.3 8.0 %collective-permute-start.6 = (bf16[1,4,4,6144]{3,2,0,1:T(4,128)(2,1)S(1)}, bf16[1,4,4,6144]{3,2,0,1:T(4,128)(2,1)S(1)}, u32[]{:S(2)}, u32[]{:S(2)}) collective-permute-start(bf16[1,4,4,6144]{3,2,0,1:T(4,128)(2,1)S(1)} %collective-permute-done.4), channel_id=1, source_target_pairs={{0,1},{1,2},{2,3},{3,4},{4,5},{5,6},{6,7},{7,0},{8,9},{9,10},{10,1... | collective-permute-start | bytes 589832 | tf_op jit(solution)/shard_map/ppermute | solution.py:20
  48.0 20.9 %all-to-all-start.2 = ((bf16[8,4,4,6144]{3,2,0,1:T(4,128)(2,1)}), bf16[8,4,4,6144]{3,2,0,1:T(4,128)(2,1)S(1)}, u32[]{:S(2)}, u32[]{:S(2)}) async-start(bf16[8,4,4,6144]{3,2,0,1:T(4,128)(2,1)} %constant_dynamic-update-slice_fusion), calls=%async_computation.3 | async-start | bytes 3145728 | tf_op jit(solution)/shard_map/all_to_all | solution.py:74
  69.0 23.1 %all-to-all-start = ((bf16[8,4,4,6144]{3,2,0,1:T(4,128)(2,1)}), bf16[8,4,4,6144]{3,2,0,1:T(4,128)(2,1)}, u32[]{:S(2)}, u32[]{:S(2)}) async-start(bf16[8,4,4,6144]{3,2,0,1:T(4,128)(2,1)} %copy.37), calls=%async_computation | async-start | bytes 3145728 | tf_op jit(solution)/shard_map/all_to_all | solution.py:73
  73.3 90.3 %reduce-scatter.3.cloned.1.call-start = ((), (), s32[]{:S(2)}) async-start(), calls=%async_computation.7 | async-start | bytes 1769472 | tf_op jit(solution)/shard_map/reduce_scatter | solution.py:85
  120.4 0.7 copy-start.3
  128.7 69.6 %reduce-scatter.5.cloned.1.call-start = ((), (), s32[]{:S(2)}) async-start(), calls=%async_computation.8 | async-start | bytes 1769472 | tf_op jit(solution)/shard_map/reduce_scatter | solution.py:111
  128.9 8.8 %copy-start.2 = (bf16[128,1024]{1,0:T(8,128)(2,1)S(1)}, bf16[128,1024]{1,0:T(8,128)(2,1)}, u32[]{:S(2)}) copy-start(bf16[128,1024]{1,0:T(8,128)(2,1)} %get-tuple-element.7) | copy-start | bytes 786436
  165.3 34.7 %all-to-all-start.1 = ((bf16[4,4,6144]{2,1,0:T(4,128)(2,1)}), bf16[4,4,6144]{2,1,0:T(4,128)(2,1)S(1)}, u32[]{:S(2)}, u32[]{:S(2)}) async-start(bf16[4,4,6144]{2,1,0:T(4,128)(2,1)} %reshape.49), calls=%async_computation.2 | async-start | bytes 393216 | tf_op jit(solution)/shard_map/all_to_all | solution.py:92
  168.8 40.7 %copy-start.1 = (bf16[6,6144]{1,0:T(8,128)(2,1)S(1)}, bf16[6,6144]{1,0:T(8,128)(2,1)}, u32[]{:S(2)}) copy-start(bf16[6,6144]{1,0:T(8,128)(2,1)} %param.10) | copy-start | bytes 221188
  200.0 8.6 %all-to-all-start.3 = ((bf16[4,4,6144]{2,1,0:T(4,128)(2,1)}), bf16[4,4,6144]{2,1,0:T(4,128)(2,1)S(1)}, u32[]{:S(2)}, u32[]{:S(2)}) async-start(bf16[4,4,6144]{2,1,0:T(4,128)(2,1)} %reshape.52), calls=%async_computation.5 | async-start | bytes 393216 | tf_op jit(solution)/shard_map/all_to_all | solution.py:120
Sparse Core Ops, SparseCore 0:
  16.4 29.9 all-gather.1
  128.8 34.7 reduce-scatter.2
  165.9 32.3 reduce-scatter.4
